TPU v7x, 32 devices: a whole 2x2x4 slice. The times are simulated.
32 devices in a mesh: parts: 2 (over x), items: 16 (over z, y, core).
Axes of the slice: x: 2, y: 2, z: 4, core: 2. Of those that a mesh axis runs over, the one named last changes fastest.
Arguments:
- user_emb: bfloat16 [4, 64, 1024], P(None, ('parts', 'items')), parts along dimension 1
- user_gate: bfloat16 [4, 64, 64], P(None, ('parts', 'items')), parts along dimension 1
- item_table: bfloat16 [16384, 1024], P(('parts', 'items')), parts along dimension 0
- item_gate: bfloat16 [16384, 64], P(('parts', 'items')), parts along dimension 0, may hold values from -6 to 6
- cand_ids: int32 [4, 8192], P(None, ('parts', 'items')), parts along dimension 1, may hold values from 0 to 8191, as said below
- positives: int32 [4, 64], P(None, 'parts'), parts along dimension 1, may hold values from 0 to 4095
- loss_weight: float32 [4, 64], P(None, 'parts'), parts along dimension 1, may hold values from 1 to 8
- w_in: float32 [64, 128], replicated, may hold values from -0.75 to 0.75
- b_in: float32 [128], replicated, may hold values from -4 to 4
- w_out: float32 [128, 8], replicated, may hold values from -1.5 to 1.5
- b_out: float32 [8], replicated, may hold values from -4 to 4
Outputs:
- user_emb_grad: float32 [4, 64, 1024], P(None, ('parts', 'items')), parts along dimension 1
- user_gate_grad: float32 [4, 64, 64], P(None, ('parts', 'items')), parts along dimension 1
- item_table_grad: float32 [16384, 1024], P(('parts', 'items')), parts along dimension 0
- item_gate_grad: float32 [16384, 64], P(('parts', 'items')), parts along dimension 0
There are 2 independent parts, one for each index of `parts`. A program takes and returns all parts, laid end to end along the dimension named above; an argument that names none is the same for every part. Nothing has to cross between parts.
Inputs may be any that keep to these rules, and one draw needn't show every extreme that they name: `cand_ids`: in each round, the ids at positions j * 256 to (j + 1) * 256 - 1 are distinct rows of the j-th block of 512 table rows.
All inputs are finite; a program needn't handle non-finite values.
Results may differ from a plain program's by a relative error of at most 0.0031.
Values may be sent and summed in bfloat16 or wider, within the bound.
A program may use at most 64 MiB of HBM per device.

v0:
```python
import math

import jax
import jax.numpy as jnp
from jax import lax
from jax.sharding import PartitionSpec as P


def forward(users, ugate_rows, items, igate_rows, w_in, b_in, w_out, b_out):
    count_u = users.shape[0]
    count_i = items.shape[0]
    comps = w_out.shape[1]
    depth = users.shape[1] // comps
    left = users.reshape(count_u, comps, depth)
    right = items.reshape(count_i, comps, depth)
    component = jnp.einsum("ukd,ikd->kui", left, right, preferred_element_type=jnp.float32) * (
        1.0 / math.sqrt(depth)
    )
    user_act = jnp.dot(ugate_rows.astype(jnp.float32), w_in, precision=lax.Precision.HIGHEST)
    item_act = jnp.dot(igate_rows.astype(jnp.float32), w_in, precision=lax.Precision.HIGHEST)
    preact = user_act[:, None, :] + item_act[None, :, :] + b_in
    hidden = jax.nn.silu(preact)
    gate_logit = (
        jnp.einsum("uih,hk->kui", hidden, w_out, precision=lax.Precision.HIGHEST)
        + b_out[:, None, None]
    )
    gates = jax.nn.softmax(gate_logit, axis=0)
    score = jnp.sum(gates * component, 0)
    return (component, gates, score, preact)


def normaliser(score):
    top = lax.pmax(jnp.max(score, 1), "items")
    total = lax.psum(jnp.sum(jnp.exp(score - top[:, None]), 1), "items")
    return (top, total)


def one_round(users, ugate_rows, items, igate_rows, pos_local, weight, w_in, b_in, w_out, b_out):
    count_u = users.shape[0]
    count_i = items.shape[0]
    comps = w_out.shape[1]
    depth = users.shape[1] // comps
    component, gates, score, preact = forward(
        users, ugate_rows, items, igate_rows, w_in, b_in, w_out, b_out
    )
    top, total = normaliser(score)
    likely = jnp.exp(score - top[:, None]) / total[:, None]
    target = (jnp.arange(count_i, dtype=jnp.int32)[None, :] == pos_local[:, None]).astype(
        jnp.float32
    )
    score_grad = weight[:, None] * (likely - target)
    comp_grad = (score_grad[None] * gates).astype(jnp.bfloat16)
    gate_grad = score_grad[None] * gates * (component - score[None])
    hidden_grad = jnp.einsum("kui,hk->uih", gate_grad, w_out, precision=lax.Precision.HIGHEST)
    sigma = jax.nn.sigmoid(preact)
    preact_grad = hidden_grad * sigma * (1.0 + preact * (1.0 - sigma))
    user_gate_part = jnp.dot(jnp.sum(preact_grad, 1), w_in.T, precision=lax.Precision.HIGHEST)
    item_gate_part = jnp.dot(jnp.sum(preact_grad, 0), w_in.T, precision=lax.Precision.HIGHEST)
    scale = 1.0 / math.sqrt(depth)
    left = users.reshape(count_u, comps, depth)
    right = items.reshape(count_i, comps, depth)
    user_part = (
        jnp.einsum("kui,ikd->ukd", comp_grad, right, preferred_element_type=jnp.float32) * scale
    )
    item_part = (
        jnp.einsum("kui,ukd->ikd", comp_grad, left, preferred_element_type=jnp.float32) * scale
    )
    return (
        user_part.reshape(count_u, comps * depth),
        user_gate_part,
        item_part.reshape(count_i, comps * depth),
        item_gate_part,
    )


def body(
    user_emb,
    user_gate,
    item_table,
    item_gate,
    cand_ids,
    positives,
    loss_weight,
    w_in,
    b_in,
    w_out,
    b_out,
):
    rounds = user_emb.shape[0]
    count_local = cand_ids.shape[1]
    table_rows = item_table.shape[0]
    local_rows = cand_ids % table_rows
    offset = lax.axis_index("items") * count_local
    table_grad = jnp.zeros((table_rows, item_table.shape[1]), jnp.float32)
    gate_table_grad = jnp.zeros((table_rows, item_gate.shape[1]), jnp.float32)
    user_grads = []
    gate_grads = []
    all_users, all_gate = (
        lax.all_gather(user_emb, "items", axis=1, tiled=True),
        lax.all_gather(user_gate, "items", axis=1, tiled=True),
    )
    for turn in range(rounds):
        users = all_users[turn]
        ugate_rows = all_gate[turn]
        rows = local_rows[turn]
        items = jnp.take(item_table, rows, axis=0)
        igate_rows = jnp.take(item_gate, rows, axis=0)
        user_part, user_gate_part, item_part, item_gate_part = one_round(
            users,
            ugate_rows,
            items,
            igate_rows,
            positives[turn] - offset,
            loss_weight[turn],
            w_in,
            b_in,
            w_out,
            b_out,
        )
        table_grad = table_grad.at[local_rows[turn]].add(item_part)
        gate_table_grad = gate_table_grad.at[local_rows[turn]].add(item_gate_part)
        user_grads.append(user_part)
        gate_grads.append(user_gate_part)
    user_result, gate_result = (
        lax.psum_scatter(jnp.stack(user_grads), "items", scatter_dimension=1, tiled=True),
        lax.psum_scatter(jnp.stack(gate_grads), "items", scatter_dimension=1, tiled=True),
    )
    return (user_result, gate_result, table_grad, gate_table_grad)


def solution(mesh):
    return jax.shard_map(
        body,
        mesh=mesh,
        in_specs=(
            P(None, ("parts", "items"), None),
            P(None, ("parts", "items"), None),
            P(("parts", "items"), None),
            P(("parts", "items"), None),
            P(None, ("parts", "items")),
            P(None, "parts"),
            P(None, "parts"),
            P(),
            P(),
            P(),
            P(),
        ),
        out_specs=(
            P(None, ("parts", "items"), None),
            P(None, ("parts", "items"), None),
            P(("parts", "items"), None),
            P(("parts", "items"), None),
        ),
        check_vma=False,
    )
```

profile of v0, /device:TPU:0, one launch (start us, length us, event | category | flops | bytes accessed | tf_op | source)
XLA Modules:
  0.0 335.8 jit_solution(1214041444890077519)
XLA Ops:
  9.1 2.0 gather_fusion.6
  11.9 1.2 gather_fusion.4
  14.0 1.2 gather_fusion.2
  15.1 1.5 gather_fusion.3
  16.7 1.2 gather_fusion
  17.9 1.5 gather_fusion.1
  19.4 23.8 %all_gather.7 = bf16[4,32,1024]{2,0,1:T(4,128)(2,1)S(1)} all-gather(bf16[4,2,1024]{2,0,1:T(4,128)(2,1)S(1)} %copy.142), channel_id=1, replica_groups=mesh['parts'=2,'items'=16] {'items'}, dimensions={1}, use_global_device_ids=true | all-gather | bytes 278528 | tf_op jit(solution)/shard_map/all_gather | solution.py:99
  43.2 1.7 slice_reduce_fusion.3
  44.9 17.5 %all_gather.6 = bf16[4,32,64]{2,0,1:T(4,128)(2,1)S(1)} all-gather(bf16[4,2,64]{2,0,1:T(4,128)(2,1)S(1)} %copy.139), channel_id=1, replica_groups=mesh['parts'=2,'items'=16] {'items'}, dimensions={1}, use_global_device_ids=true | all-gather | bytes 17408 | tf_op jit(solution)/shard_map/all_gather | solution.py:100
  63.5 4.5 %fusion.57 = f32[8,32,256]{2,0,1:T(8,128)S(1)} fusion(f32[256,128]{1,0:T(8,128)S(1)} %fusion.132, f32[32,128]{1,0:T(8,128)S(1)} %fusion.160, f32[128]{0:T(128)S(1)} %copy-done.76, f32[8]{0:T(128)S(1)} %copy-done.74, f32[128,8]{0,1:T(8,128)S(1)} %copy-done.71), kind=kOutput, calls=%fused_computation.75 | convolution fusion | flops 107020288 | bytes 414240 | tf_op jit(solution)/shard_map/uih,hk->kui/dot_general | solution.py:24
  68.1 12.3 %fusion.191 = (f32[32,256]{1,0:T(8,128)S(1)}, f32[8,32,256]{2,0,1:T(8,128)S(1)}) fusion(f32[8,32,256]{2,0,1:T(8,128)S(1)} %fusion.57), kind=kOutput, calls=%fused_computation.286 | output fusion | flops 131079 | bytes 557056 | tf_op jit(solution)/shard_map/sub | solution.py:27
  81.8 4.5 %fusion.51 = f32[8,32,256]{2,0,1:T(8,128)S(1)} fusion(f32[256,128]{1,0:T(8,128)S(1)} %fusion.134, f32[32,128]{1,0:T(8,128)S(1)} %fusion.161, f32[128]{0:T(128)S(1)} %copy-done.76, f32[8]{0:T(128)S(1)} %copy-done.74, f32[128,8]{0,1:T(8,128)S(1)} %copy-done.71), kind=kOutput, calls=%fused_computation.73 | convolution fusion | flops 107020288 | bytes 414240 | tf_op jit(solution)/shard_map/uih,hk->kui/dot_general | solution.py:24
  86.3 1.9 fusion.192
  91.8 1.1 fusion.136
  93.6 5.2 %fusion.45 = f32[8,32,256]{2,0,1:T(8,128)S(1)} fusion(f32[256,128]{1,0:T(8,128)S(1)} %fusion.136, f32[32,128]{1,0:T(8,128)S(1)} %fusion.162, f32[128]{0:T(128)} %param.23, f32[8]{0:T(128)} %param.25, f32[128,8]{0,1:T(8,128)} %param.24), kind=kOutput, calls=%fused_computation.71 | convolution fusion | flops 107020288 | bytes 414240 | tf_op jit(solution)/shard_map/uih,hk->kui/dot_general | solution.py:24
  98.9 1.9 fusion.193
  102.1 4.5 %fusion.39 = f32[8,32,256]{2,0,1:T(8,128)S(1)} fusion(f32[128]{0:T(128)S(1)} %copy-done.77, f32[256,128]{1,0:T(8,128)S(1)} %fusion.138, f32[32,128]{1,0:T(8,128)S(1)} %fusion.163, f32[8]{0:T(128)S(1)} %copy-done.75, f32[128,8]{0,1:T(8,128)S(1)} %copy-done.72), kind=kOutput, calls=%fused_computation.69 | convolution fusion | flops 107020288 | bytes 414240 | tf_op jit(solution)/shard_map/uih,hk->kui/dot_general | solution.py:24
  106.7 1.9 fusion.194
  110.0 31.1 %all-reduce.3 = (f32[32]{0:T(128)S(1)}, f32[32]{0:T(128)S(1)}, f32[32]{0:T(128)S(1)}, f32[32]{0:T(128)S(1)}) all-reduce(f32[32]{0:T(128)S(1)} %reduce_max.79, f32[32]{0:T(128)S(1)} %copy-done.63, f32[32]{0:T(128)S(1)} %reduce_max.75, f32[32]{0:T(128)S(1)} %reduce_max.73), channel_id=1, replica_groups=mesh['parts'=2,'items'=16] {'items'}, use_global_device_ids=true, to_apply=%region_25.28 | all-reduce | flops 128 | bytes 1024 | tf_op jit(solution)/shard_map/pmax | solution.py:33
  143.0 30.2 %all-reduce.2 = (f32[32]{0:T(128)S(1)}, f32[32]{0:T(128)S(1)}, f32[32]{0:T(128)}, f32[32]{0:T(128)}) all-reduce(f32[32]{0:T(128)S(1)} %fusion.159, f32[32]{0:T(128)S(1)} %fusion.158, f32[32]{0:T(128)S(1)} %fusion.157, f32[32]{0:T(128)S(1)} %fusion.156), channel_id=1, replica_groups=mesh['parts'=2,'items'=16] {'items'}, use_global_device_ids=true, to_apply=%region_27.30 | all-reduce | flops 128 | bytes 1024 | tf_op jit(solution)/shard_map/psum | solution.py:34
  174.5 1.4 fusion.60
  177.5 1.4 fusion.61
  179.6 1.6 stack_reshape.14
  181.2 1.5 subtract_multiply_fusion.2
  186.2 1.1 fusion.63
  188.4 1.2 copy.173
  189.7 9.4 %fusion.185 = (f32[256,128]{1,0:T(8,128)}, f32[32,128]{1,0:T(8,128)S(1)}) fusion(f32[128]{0:T(128)S(1)} %copy-done.78, f32[256,128]{1,0:T(8,128)} %copy-done.45, f32[32,128]{1,0:T(8,128)} %copy-done.55, f32[128,8]{0,1:T(8,128)S(1)} %copy-done.73, f32[8,256,32]{1,2,0:T(8,128)} %copy-done.36, f32[32,256]{1,0:T(8,128)S(1)} %fusion.86, ...), kind=kOutput, calls=%fused_computation.280 | convolution fusion | flops 113537024 | bytes 922112 | tf_op jit(solution)/shard_map/kui,hk->uih/dot_general | solution.py:54
  199.2 8.5 %fusion.186 = (f32[256,128]{1,0:T(8,128)}, f32[32,128]{1,0:T(8,128)S(1)}) fusion(f32[128]{0:T(128)S(1)} %copy-done.78, f32[256,128]{1,0:T(8,128)S(1)} %copy-done.47, f32[32,128]{1,0:T(8,128)S(1)} %copy-done.57, f32[128,8]{0,1:T(8,128)S(1)} %copy-done.73, f32[8,256,32]{1,2,0:T(8,128)S(1)} %copy-done.33, f32[32,256]{1,0:T(8,128)S(1)} %fusion.89, ...), kind=kOutput, calls=%fused_computation.281 | convolution fusion | flops 113537024 | bytes 922112 | tf_op jit(solution)/shard_map/kui,hk->uih/dot_general | solution.py:54
  207.8 8.9 %fusion.187 = (f32[256,128]{1,0:T(8,128)}, f32[32,128]{1,0:T(8,128)S(1)}) fusion(f32[128]{0:T(128)S(1)} %copy-done.78, f32[256,128]{1,0:T(8,128)S(1)} %copy-done.49, f32[32,128]{1,0:T(8,128)S(1)} %copy-done.59, f32[128,8]{0,1:T(8,128)S(1)} %copy-done.73, f32[8,256,32]{1,2,0:T(8,128)S(1)} %copy-done.35, f32[32,256]{1,0:T(8,128)S(1)} %fusion.92, ...), kind=kOutput, calls=%fused_computation.282 | convolution fusion | flops 113537024 | bytes 922112 | tf_op jit(solution)/shard_map/kui,hk->uih/dot_general | solution.py:54
  216.7 8.5 %fusion.188 = (f32[256,128]{1,0:T(8,128)}, f32[32,128]{1,0:T(8,128)S(1)}) fusion(f32[128]{0:T(128)S(1)} %copy-done.78, f32[256,128]{1,0:T(8,128)S(1)} %copy-done.51, f32[32,128]{1,0:T(8,128)S(1)} %copy-done.61, f32[128,8]{0,1:T(8,128)S(1)} %copy-done.73, f32[8,256,32]{1,2,0:T(8,128)S(1)} %copy-done.38, f32[32,256]{1,0:T(8,128)S(1)} %copy-done.12, ...), kind=kOutput, calls=%fused_computation.283 | convolution fusion | flops 113537024 | bytes 922112 | tf_op jit(solution)/shard_map/kui,hk->uih/dot_general | solution.py:54
  226.0 1.3 convolution_multiply_fusion.1
  227.3 1.4 convolution_multiply_fusion
  229.5 58.0 %all-reduce.1 = f32[4,32,64]{2,0,1:T(4,128)S(1)} all-reduce(f32[4,32,64]{2,0,1:T(4,128)S(1)} %copy.174), channel_id=3, replica_groups=mesh['parts'=2,'items'=16] {'items'}, use_global_device_ids=true, to_apply=%region_33.36.clone | all-reduce | flops 8192 | bytes 65536
  287.5 1.8 fusion.195
  289.3 1.8 fusion.196
  293.9 1.3 copy.177
  295.2 1.3 copy.180
  296.5 1.3 copy.183
  297.8 1.4 copy.186
  299.2 3.8 %scatter_custom_fusion = f32[512,1024]{1,0:T(8,128)S(1)} fusion(s32[256]{0:T(256)S(1)} %bitcast.284, f32[256,1024]{1,0:T(8,128)} %copy.177, f32[]{:T(128)} %constant.35.clone.1), kind=kCustom, calls=%fused_computation.88 | custom fusion | flops 262144 | bytes 2097664 | tf_op jit(solution)/shard_map/scatter-add | solution.py:120
  303.0 1.9 scatter_custom_fusion.4
  304.9 2.4 scatter_fusion.3
  307.3 2.4 scatter_fusion.4
  309.7 1.8 fusion.198
  311.5 2.4 scatter_fusion.5
  314.7 4.1 %scatter_fusion = f32[512,1024]{1,0:T(8,128)S(1)} fusion(f32[512,1024]{1,0:T(8,128)S(1)} %scatter_custom_fusion, s32[256]{0:T(256)S(1)} %bitcast.275, f32[256,1024]{1,0:T(8,128)} %copy.180), kind=kCustom, calls=%fused_computation.9 | custom fusion | flops 262144 | bytes 3146752 | tf_op jit(solution)/shard_map/scatter-add | solution.py:120
  318.8 4.3 %scatter_fusion.1 = f32[512,1024]{1,0:T(8,128)S(1)} fusion(f32[512,1024]{1,0:T(8,128)S(1)} %scatter_fusion, s32[256]{0:T(256)S(1)} %bitcast.273, f32[256,1024]{1,0:T(8,128)} %copy.183), kind=kCustom, calls=%fused_computation.10 | custom fusion | flops 262144 | bytes 3146752 | tf_op jit(solution)/shard_map/scatter-add | solution.py:120
  323.1 4.1 %scatter_fusion.2 = f32[512,1024]{1,0:T(8,128)S(1)} fusion(f32[512,1024]{1,0:T(8,128)S(1)} %scatter_fusion.1, s32[256]{0:T(256)S(1)} %bitcast.271, f32[256,1024]{1,0:T(8,128)} %copy.186), kind=kCustom, calls=%fused_computation.11 | custom fusion | flops 262144 | bytes 3146752 | tf_op jit(solution)/shard_map/scatter-add | solution.py:120
  (238 shorter events, 28.9 us)
Async XLA Ops:
  7.2 320.1 %all-reduce.6.cloned.1.call-start = ((), (), s32[]{:S(2)}) async-start(), calls=%async_computation | async-start | bytes 1048576
  8.0 80.2 %copy-start.70 = (pred[256]{0:T(512)(128)(4,1)}, pred[256]{0:T(512)(128)(4,1)S(1)}, u32[]{:S(2)}) copy-start(pred[256]{0:T(512)(128)(4,1)S(1)} %compare_and_fusion) | copy-start | bytes 772
  8.1 81.6 %copy-start.69 = (pred[256]{0:T(512)(128)(4,1)}, pred[256]{0:T(512)(128)(4,1)S(1)}, u32[]{:S(2)}) copy-start(pred[256]{0:T(512)(128)(4,1)S(1)} %compare_and_fusion.1) | copy-start | bytes 772
  13.1 76.7 %copy-start.5 = (bf16[256,1024]{1,0:T(8,128)(2,1)}, bf16[256,1024]{1,0:T(8,128)(2,1)S(1)}, u32[]{:S(2)}) copy-start(bf16[256,1024]{1,0:T(8,128)(2,1)S(1)} %gather_fusion.4) | copy-start | bytes 1572868
  13.9 86.9 %copy-start.67 = (pred[256]{0:T(512)(128)(4,1)}, pred[256]{0:T(512)(128)(4,1)S(1)}, u32[]{:S(2)}) copy-start(pred[256]{0:T(512)(128)(4,1)S(1)} %compare_and_fusion.2) | copy-start | bytes 772
  16.6 91.9 %copy-start.68 = (pred[256]{0:T(512)(128)(4,1)}, pred[256]{0:T(512)(128)(4,1)S(1)}, u32[]{:S(2)}) copy-start(pred[256]{0:T(512)(128)(4,1)S(1)} %compare_and_fusion.3) | copy-start | bytes 772
  16.7 28.2 %copy-start.64 = (bf16[4,2,64]{2,1,0:T(2,128)(2,1)S(1)}, bf16[4,2,64]{2,1,0:T(2,128)(2,1)}, u32[]{:S(2)}) copy-start(bf16[4,2,64]{2,1,0:T(2,128)(2,1)} %param.16) | copy-start | bytes 3076
  16.7 46.4 %copy-start.2 = (f32[64,128]{1,0:T(8,128)S(1)}, f32[64,128]{1,0:T(8,128)}, u32[]{:S(2)}) copy-start(f32[64,128]{1,0:T(8,128)} %param.22) | copy-start | bytes 98308
  17.9 45.6 %copy-start.71 = (f32[128,8]{0,1:T(8,128)S(1)}, f32[128,8]{0,1:T(8,128)}, u32[]{:S(2)}) copy-start(f32[128,8]{0,1:T(8,128)} %param.24) | copy-start | bytes 12292
  17.9 45.6 %copy-start.74 = (f32[8]{0:T(128)S(1)}, f32[8]{0:T(128)}, u32[]{:S(2)}) copy-start(f32[8]{0:T(128)} %param.25) | copy-start | bytes 100
  17.9 45.6 %copy-start.76 = (f32[128]{0:T(128)S(1)}, f32[128]{0:T(128)}, u32[]{:S(2)}) copy-start(f32[128]{0:T(128)} %param.23) | copy-start | bytes 1540
  44.9 43.4 %copy-start.23 = (bf16[32,1024]{1,0:T(8,128)(2,1)}, bf16[32,1024]{1,0:T(8,128)(2,1)S(1)}, u32[]{:S(2)}) copy-start(bf16[32,1024]{1,0:T(8,128)(2,1)S(1)} %get-tuple-element.27) | copy-start | bytes 196612
  44.9 44.8 %copy-start.25 = (bf16[32,1024]{1,0:T(8,128)(2,1)}, bf16[32,1024]{1,0:T(8,128)(2,1)S(1)}, u32[]{:S(2)}) copy-start(bf16[32,1024]{1,0:T(8,128)(2,1)S(1)} %get-tuple-element.28) | copy-start | bytes 196612
  44.9 55.9 %copy-start.27 = (bf16[32,1024]{1,0:T(8,128)(2,1)}, bf16[32,1024]{1,0:T(8,128)(2,1)S(1)}, u32[]{:S(2)}) copy-start(bf16[32,1024]{1,0:T(8,128)(2,1)S(1)} %get-tuple-element.29) | copy-start | bytes 196612
  63.2 4.9 %copy-start.55 = (f32[32,128]{1,0:T(8,128)}, f32[32,128]{1,0:T(8,128)S(1)}, u32[]{:S(2)}) copy-start(f32[32,128]{1,0:T(8,128)S(1)} %fusion.160) | copy-start | bytes 49156
  80.4 93.5 %copy-start.15 = (f32[32,256]{1,0:T(8,128)}, f32[32,256]{1,0:T(8,128)S(1)}, u32[]{:S(2)}) copy-start(f32[32,256]{1,0:T(8,128)S(1)} %get-tuple-element.58) | copy-start | bytes 98308
  81.8 6.5 %copy-start.6 = (bf16[256,1024]{1,0:T(8,128)(2,1)S(1)}, bf16[256,1024]{1,0:T(8,128)(2,1)}, u32[]{:S(2)}) copy-start(bf16[256,1024]{1,0:T(8,128)(2,1)} %gather_fusion.6) | copy-start | bytes 1572868
  86.3 5.4 %copy-start.54 = (bf16[1,32,64]{2,0,1:T(2,128)(2,1)S(1)}, bf16[1,32,64]{2,0,1:T(2,128)(2,1)}, u32[]{:S(2)}) copy-start(bf16[1,32,64]{2,0,1:T(2,128)(2,1)} %get-tuple-element.40) | copy-start | bytes 12292
  88.2 10.6 %copy-start.17 = (f32[32,256]{1,0:T(8,128)}, f32[32,256]{1,0:T(8,128)S(1)}, u32[]{:S(2)}) copy-start(f32[32,256]{1,0:T(8,128)S(1)} %get-tuple-element.60) | copy-start | bytes 98308
  100.8 5.8 %copy-start.19 = (f32[32,256]{1,0:T(8,128)}, f32[32,256]{1,0:T(8,128)S(1)}, u32[]{:S(2)}) copy-start(f32[32,256]{1,0:T(8,128)S(1)} %get-tuple-element.62) | copy-start | bytes 98308
  101.7 4.9 %copy-start.60 = (f32[32,128]{1,0:T(8,128)}, f32[32,128]{1,0:T(8,128)S(1)}, u32[]{:S(2)}) copy-start(f32[32,128]{1,0:T(8,128)S(1)} %fusion.163) | copy-start | bytes 49156
  102.0 6.5 %copy-start.29 = (bf16[32,1024]{1,0:T(8,128)(2,1)S(1)}, bf16[32,1024]{1,0:T(8,128)(2,1)}, u32[]{:S(2)}) copy-start(bf16[32,1024]{1,0:T(8,128)(2,1)} %get-tuple-element.26) | copy-start | bytes 196612
  106.6 35.2 %copy-start.65 = (f32[4,32]{1,0:T(4,128)S(1)}, f32[4,32]{1,0:T(4,128)}, u32[]{:S(2)}) copy-start(f32[4,32]{1,0:T(4,128)} %param.21) | copy-start | bytes 1540
  106.6 35.8 %copy-start.66 = (s32[4,32]{1,0:T(4,128)S(1)}, s32[4,32]{1,0:T(4,128)}, u32[]{:S(2)}) copy-start(s32[4,32]{1,0:T(4,128)} %param.20) | copy-start | bytes 1540
  108.5 65.5 %copy-start.21 = (f32[32,256]{1,0:T(8,128)}, f32[32,256]{1,0:T(8,128)S(1)}, u32[]{:S(2)}) copy-start(f32[32,256]{1,0:T(8,128)S(1)} %get-tuple-element.64) | copy-start | bytes 98308
  109.9 64.1 %copy-start.11 = (f32[32,256]{1,0:T(8,128)}, f32[32,256]{1,0:T(8,128)S(1)}, u32[]{:S(2)}) copy-start(f32[32,256]{1,0:T(8,128)S(1)} %fusion.95) | copy-start | bytes 98308
  189.6 9.5 %copy-start.18 = (f32[32,256]{1,0:T(8,128)S(1)}, f32[32,256]{1,0:T(8,128)}, u32[]{:S(2)}) copy-start(f32[32,256]{1,0:T(8,128)} %copy-done.17) | copy-start | bytes 98308
  189.6 9.5 %copy-start.33 = (f32[8,256,32]{1,2,0:T(8,128)S(1)}, f32[8,256,32]{1,2,0:T(8,128)}, u32[]{:S(2)}) copy-start(f32[8,256,32]{1,2,0:T(8,128)} %copy-done.32) | copy-start | bytes 786436
  189.7 9.5 %copy-start.39 = (f32[32,256]{1,0:T(8,128)S(1)}, f32[32,256]{1,0:T(8,128)}, u32[]{:S(2)}) copy-start(f32[32,256]{1,0:T(8,128)} %get-tuple-element.67) | copy-start | bytes 98308
  189.7 9.5 %copy-start.47 = (f32[256,128]{1,0:T(8,128)S(1)}, f32[256,128]{1,0:T(8,128)}, u32[]{:S(2)}) copy-start(f32[256,128]{1,0:T(8,128)} %copy-done.46) | copy-start | bytes 393220
  189.7 9.5 %copy-start.57 = (f32[32,128]{1,0:T(8,128)S(1)}, f32[32,128]{1,0:T(8,128)}, u32[]{:S(2)}) copy-start(f32[32,128]{1,0:T(8,128)} %copy-done.56) | copy-start | bytes 49156
  199.2 8.5 %copy-start.20 = (f32[32,256]{1,0:T(8,128)S(1)}, f32[32,256]{1,0:T(8,128)}, u32[]{:S(2)}) copy-start(f32[32,256]{1,0:T(8,128)} %copy-done.19) | copy-start | bytes 98308
  199.2 8.5 %copy-start.35 = (f32[8,256,32]{1,2,0:T(8,128)S(1)}, f32[8,256,32]{1,2,0:T(8,128)}, u32[]{:S(2)}) copy-start(f32[8,256,32]{1,2,0:T(8,128)} %copy-done.34) | copy-start | bytes 786436
  199.2 8.5 %copy-start.44 = (f32[32,256]{1,0:T(8,128)S(1)}, f32[32,256]{1,0:T(8,128)}, u32[]{:S(2)}) copy-start(f32[32,256]{1,0:T(8,128)} %copy-done.43) | copy-start | bytes 98308
  199.2 8.5 %copy-start.49 = (f32[256,128]{1,0:T(8,128)S(1)}, f32[256,128]{1,0:T(8,128)}, u32[]{:S(2)}) copy-start(f32[256,128]{1,0:T(8,128)} %copy-done.48) | copy-start | bytes 393220
  199.2 8.5 %copy-start.59 = (f32[32,128]{1,0:T(8,128)S(1)}, f32[32,128]{1,0:T(8,128)}, u32[]{:S(2)}) copy-start(f32[32,128]{1,0:T(8,128)} %copy-done.58) | copy-start | bytes 49156
  207.7 8.9 %copy-start.12 = (f32[32,256]{1,0:T(8,128)S(1)}, f32[32,256]{1,0:T(8,128)}, u32[]{:S(2)}) copy-start(f32[32,256]{1,0:T(8,128)} %copy-done.11) | copy-start | bytes 98308
  207.7 8.9 %copy-start.22 = (f32[32,256]{1,0:T(8,128)S(1)}, f32[32,256]{1,0:T(8,128)}, u32[]{:S(2)}) copy-start(f32[32,256]{1,0:T(8,128)} %copy-done.21) | copy-start | bytes 98308
  207.7 8.9 %copy-start.38 = (f32[8,256,32]{1,2,0:T(8,128)S(1)}, f32[8,256,32]{1,2,0:T(8,128)}, u32[]{:S(2)}) copy-start(f32[8,256,32]{1,2,0:T(8,128)} %copy-done.37) | copy-start | bytes 786436
  207.7 8.9 %copy-start.42 = (f32[32,256]{1,0:T(8,128)S(1)}, f32[32,256]{1,0:T(8,128)}, u32[]{:S(2)}) copy-start(f32[32,256]{1,0:T(8,128)} %get-tuple-element.69) | copy-start | bytes 98308
  207.7 8.9 %copy-start.51 = (f32[256,128]{1,0:T(8,128)S(1)}, f32[256,128]{1,0:T(8,128)}, u32[]{:S(2)}) copy-start(f32[256,128]{1,0:T(8,128)} %copy-done.50) | copy-start | bytes 393220
  207.7 8.9 %copy-start.61 = (f32[32,128]{1,0:T(8,128)S(1)}, f32[32,128]{1,0:T(8,128)}, u32[]{:S(2)}) copy-start(f32[32,128]{1,0:T(8,128)} %copy-done.60) | copy-start | bytes 49156
  216.7 8.5 %copy-start.10 = (bf16[8,32,256]{2,0,1:T(8,128)(2,1)S(1)}, bf16[8,32,256]{2,0,1:T(8,128)(2,1)}, u32[]{:S(2)}) copy-start(bf16[8,32,256]{2,0,1:T(8,128)(2,1)} %copy-done.9) | copy-start | bytes 393220
  216.7 8.5 %copy-start.30 = (bf16[32,1024]{1,0:T(8,128)(2,1)S(1)}, bf16[32,1024]{1,0:T(8,128)(2,1)}, u32[]{:S(2)}) copy-start(bf16[32,1024]{1,0:T(8,128)(2,1)} %get-tuple-element.26) | copy-start | bytes 196612
  216.7 8.9 %copy-start.8 = (bf16[8,32,256]{2,0,1:T(8,128)(2,1)S(1)}, bf16[8,32,256]{2,0,1:T(8,128)(2,1)}, u32[]{:S(2)}) copy-start(bf16[8,32,256]{2,0,1:T(8,128)(2,1)} %copy-done.7) | copy-start | bytes 393220
  216.7 8.9 %copy-start.28 = (bf16[32,1024]{1,0:T(8,128)(2,1)S(1)}, bf16[32,1024]{1,0:T(8,128)(2,1)}, u32[]{:S(2)}) copy-start(bf16[32,1024]{1,0:T(8,128)(2,1)} %copy-done.27) | copy-start | bytes 196612
  226.0 66.0 %copy-start.79 = (u32[32]{0:T(128)S(1)}, u32[32]{0:T(128)}, u32[]{:S(2)}) copy-start(u32[32]{0:T(128)} %constant.65) | copy-start | bytes 388
  227.3 63.8 %copy-start.52 = (f32[256,128]{1,0:T(8,128)S(1)}, f32[256,128]{1,0:T(8,128)}, u32[]{:S(2)}) copy-start(f32[256,128]{1,0:T(8,128)} %get-tuple-element.20) | copy-start | bytes 393220
  (33 other events, 69.3 us)
Sparse Core Ops, SparseCore 0:
  189.7 87.3 all-reduce.5
where the time goes:
time: 339 us; the launch traced here: 336 us
  blocking collectives  161 us (47%)
  matrix products  73.2 us (22%)
  other arithmetic  53 us (16%)
  local copies, waits for them, and re-layouts  32.7 us (10%)
  between operations  16.2 us (5%)
    unnamed x1, blocking collectives  58 us
    dot_general x4, matrix products, one_round(): jnp.einsum('kui,hk->uih', gate_grad, w_out, precision=lax.Precision.HIGHEST)  35.2 us
    pmax x1, blocking collectives, normaliser(): top = lax.pmax(jnp.max(score, 1), 'items')  31.1 us
    psum x1, blocking collectives, normaliser(): total = lax.psum(jnp.sum(jnp.exp(score - top[:, None]), 1), 'items')  30.2 us
    all_gather x1, blocking collectives, body(): lax.all_gather(user_emb, 'items', axis=1, tiled=True)  23.8 us
    dot_general x4, matrix products, forward(): jnp.einsum('uih,hk->kui', hidden, w_out, precision=lax.Precision.HIGHEST)  18.8 us
    sub x4, other arithmetic, forward(): gates = jax.nn.softmax(gate_logit, axis=0)  17.9 us
    all_gather x1, blocking collectives, body(): lax.all_gather(user_gate, 'items', axis=1, tiled=True)  17.5 us
  transfers between devices with their start and end apart: 1, of which 0 were waited for; matrix products, arithmetic and copies ran while one was open for 23% of the time, Pallas kernels for 0%

commit v1 on v0

v1 whole, which is shorter than its diff:
```python
import functools
import math

import jax
import jax.numpy as jnp
from jax import lax
from jax.experimental import pallas as pl
from jax.experimental.pallas import tpu as pltpu
from jax.sharding import PartitionSpec as P

MESH = pl.DeviceIdType.MESH
F32 = jnp.float32
BF16 = jnp.bfloat16


def mm(a, b):
    return jnp.dot(a, b, preferred_element_type=F32)


def mm_nt(a, b):
    return lax.dot_general(a, b, (((1,), (1,)), ((), ())), preferred_element_type=F32)


def split(x):
    hi = x.astype(BF16)
    return hi, (x - hi.astype(F32)).astype(BF16)


def iota(shape, dim):
    return lax.broadcasted_iota(jnp.int32, shape, dim)


def to_col(row, rows):
    lanes = row.shape[1]
    keep = iota((rows, lanes), 0) == iota((rows, lanes), 1)
    return jnp.sum(jnp.where(keep, jnp.broadcast_to(row, (rows, lanes)), 0.0), 1, keepdims=True)


def to_row(col, lanes):
    rows = col.shape[0]
    keep = iota((rows, lanes), 0) == iota((rows, lanes), 1)
    return jnp.sum(jnp.where(keep, jnp.broadcast_to(col, (rows, lanes)), 0.0), 0, keepdims=True)


def kernel(
    n,
    dims,
    x_ref,
    tab_ref,
    ig_ref,
    ids_ref,
    pos_ref,
    lw_ref,
    win_ref,
    bin_ref,
    wout_ref,
    bout_ref,
    zo_ref,
    ugo_ref,
    tg_ref,
    gt_ref,
    ru,
    ubig,
    vals,
    iact,
    uact,
    comp_s,
    gate_s,
    score_s,
    st_out,
    st_in,
    ggt,
    cgt,
    si,
    up,
    us,
    zs,
    rz,
    ugs,
    rug,
    u_ss,
    u_rs,
    s_ss,
    s_rs,
    z_ss,
    z_rs,
    g_ss,
    g_rs,
):
    R, NU, UL, C, T, K, E, G, H = dims
    D = E // K
    HALF = E // 2
    scale = 1.0 / math.sqrt(D)
    me = lax.axis_index("items")

    def each_peer(make, act):
        def step(d, carry):
            act(make(d, lax.rem(me + d, n)))
            return carry

        lax.fori_loop(1, n, step, 0)

    def users_copy(d, peer):
        return pltpu.make_async_remote_copy(
            x_ref, ru.at[me], u_ss.at[d], u_rs.at[d], device_id={"items": peer}, device_id_type=MESH
        )

    def stats_copy(r):
        return lambda d, peer: pltpu.make_async_remote_copy(
            st_out.at[r],
            st_in.at[r, me],
            s_ss.at[r, d],
            s_rs.at[r, d],
            device_id={"items": peer},
            device_id_type=MESH,
        )

    def grads_copy(r):
        return lambda d, peer: pltpu.make_async_remote_copy(
            zs.at[r, peer],
            rz.at[r, me],
            z_ss.at[r, d],
            z_rs.at[r, d],
            device_id={"items": peer},
            device_id_type=MESH,
        )

    def gates_copy(d, peer):
        return pltpu.make_async_remote_copy(
            ugs.at[peer], rug.at[me], g_ss.at[d], g_rs.at[d], device_id={"items": peer}, device_id_type=MESH
        )

    def start(c):
        c.start()

    def wait_recv(c):
        c.wait_recv()

    def wait_send(c):
        c.wait_send()

    barrier = pltpu.get_barrier_semaphore()

    def greet(d, carry):
        pl.semaphore_signal(barrier, inc=1, device_id={"items": lax.rem(me + d, n)}, device_id_type=MESH)
        return carry

    lax.fori_loop(1, n, greet, 0)
    pl.semaphore_wait(barrier, n - 1)
    each_peer(users_copy, start)
    ru[me] = x_ref[...]

    w_in = win_ref[...]
    wi_hi, wi_lo = split(w_in)

    def onehot_cols(r):
        row = ids_ref[pl.ds(r, 1), :] - me * T
        return (iota((T, C), 0) == jnp.broadcast_to(row, (T, C))).astype(F32).astype(BF16)

    for r in range(R):
        row = (ids_ref[pl.ds(r, 1), :] - me * T).astype(F32)
        col = to_col(row, C).astype(jnp.int32)
        pick = (iota((C, T), 1) == jnp.broadcast_to(col, (C, T))).astype(F32).astype(BF16)
        vals[r] = mm(pick, tab_ref[...]).astype(BF16)
        q = mm(pick, ig_ref[...]).astype(BF16)
        iact[r] = 0.5 * (mm(q, wi_hi) + mm(q, wi_lo))

    each_peer(users_copy, wait_recv)

    packed = ru[...].reshape(n * 16, HALF + 128)
    rows = iota((R * NU, n * 16), 0)
    cols = iota((R * NU, n * 16), 1)
    turn, user = rows // NU, rows % NU
    where_to = (user // UL) * 16 + turn * UL + user % UL
    first = mm((cols == where_to).astype(F32).astype(BF16), packed)
    second = mm((cols == where_to + 8).astype(F32).astype(BF16), packed[:, :HALF])
    ug = first[:, HALF : HALF + G].astype(BF16)
    uact[...] = 0.5 * (mm(ug, wi_hi) + mm(ug, wi_lo) + bin_ref[...])
    for r in range(R):
        for half, part in enumerate((first[:, :HALF], second)):
            rows_r = part[r * NU : (r + 1) * NU]
            wide = jnp.broadcast_to(rows_r[:, None, :], (NU, K, HALF))
            mine = iota((NU, K, HALF), 1) == (iota((NU, K, HALF), 2) + half * HALF) // D
            ubig[r, :, half * HALF : (half + 1) * HALF] = (
                jnp.where(mine, wide, 0.0).reshape(NU * K, HALF).astype(BF16)
            )

    w_out = wout_ref[...]
    wo_hi = w_out.astype(BF16).astype(F32)
    wo_lo = w_out - wo_hi
    logit_w = jnp.concatenate(
        [jnp.concatenate([wo_hi, wo_hi], 1), jnp.concatenate([wo_lo, wo_lo], 1)], 0
    ).astype(BF16)
    b_col = to_col(bout_ref[...], K)

    STEP = 4
    for r in range(R):

        def fwd(i, carry, r=r):
            for s in range(STEP):
                u = i * STEP + s
                y = iact[r] + uact[pl.ds(r * NU + u, 1), :]
                t = jnp.tanh(y)
                h = y + y * t
                hi, lo = split(h)
                lg = mm_nt(logit_w, jnp.concatenate([hi, lo], 1))
                gate_s[r, pl.ds(pl.multiple_of(u * K, K), K), :] = lg[:K] + lg[K:] + b_col
            return carry

        lax.fori_loop(0, NU // STEP, fwd, 0)
        comp = (mm_nt(ubig[r], vals[r]) * scale).reshape(NU, K, C)
        lg = gate_s[r].reshape(NU, K, C)
        p = jnp.exp(lg - jnp.max(lg, 1, keepdims=True))
        gates = p / jnp.sum(p, 1, keepdims=True)
        score = jnp.sum(gates * comp, 1)
        comp_s[r] = comp.reshape(NU * K, C)
        gate_s[r] = gates.reshape(NU * K, C)
        score_s[r] = score
        ltop = jnp.max(score, 1, keepdims=True)
        ltot = jnp.sum(jnp.exp(score - ltop), 1, keepdims=True)
        st = jnp.where(iota((8, 128), 0) == 0, to_row(ltop, 128), to_row(ltot, 128))
        st_out[r] = st
        st_in[r, me] = st
        each_peer(stats_copy(r), start)

    whid = jnp.concatenate([wo_hi, wo_hi, wo_lo, wo_lo], 0) * 0.5
    whid = jnp.concatenate([whid] * 4, 0)
    whid = jnp.concatenate([whid] * 4, 1)
    keep = iota((16 * K, 4 * H), 0) // (4 * K) == iota((16 * K, 4 * H), 1) // H
    whid = jnp.where(keep, whid, 0.0).astype(BF16)
    eye = (iota((C, C), 0) == iota((C, C), 1)).astype(F32).astype(BF16)
    CH = 64
    gt_total = jnp.zeros((T, G), F32)
    for r in range(R):
        each_peer(stats_copy(r), wait_recv)
        st = st_in[r]
        tops, tots = st[:, 0, :], st[:, 1, :]
        top = jnp.max(tops, 0, keepdims=True)
        tot = jnp.sum(tots * jnp.exp(tops - top), 0, keepdims=True)
        top_c = to_col(top, NU)
        tot_c = to_col(tot, NU)
        w_c = to_col(lw_ref[pl.ds(r, 1), :], NU)
        pos_c = to_col((pos_ref[pl.ds(r, 1), :] - me * C).astype(F32), NU).astype(jnp.int32)
        score = score_s[r]
        hit = (iota((NU, C), 1) == pos_c).astype(F32)
        sg = w_c * (jnp.exp(score - top_c) / tot_c - hit)
        cg = sg[:, None, :] * gate_s[r].reshape(NU, K, C)
        gg = cg * (comp_s[r].reshape(NU, K, C) - score[:, None, :])
        cgb = cg.reshape(NU * K, C).astype(BF16)
        g_hi = gg.astype(BF16).astype(F32)
        g_lo = gg - g_hi
        g4 = jnp.concatenate([g_hi, g_lo, g_hi, g_lo], 1).reshape(NU * 4 * K, C).astype(BF16)
        ggt[...] = mm_nt(eye, g4).astype(BF16)

        wide = mm(cgb, vals[r])
        kk = iota((NU * K, D), 0) % K
        z = jnp.zeros((NU * K, D), F32)
        for k in range(K):
            z = jnp.where(kk == k, wide[:, k * D : (k + 1) * D], z)
        zb = (z * scale).astype(BF16).reshape(n, UL * K, D)
        zs[r] = zb
        rz[r, me] = zs[r, me]
        each_peer(grads_copy(r), start)

        hot = onehot_cols(r)
        cgt[r] = mm_nt(hot, cgb).astype(BF16)

        si[...] = jnp.zeros_like(si)

        def bwd(i, carry, r=r):
            sums = [jnp.zeros((8, H), F32) for _ in range(4)]
            lanes = pl.ds(pl.multiple_of(i * 128, 128), 128)
            for c in range(C // CH):
                at = pl.ds(c * CH, CH)
                hg = mm(ggt[at, lanes], whid)
                total = None
                for s in range(4):
                    y = iact[r, at, :] + uact[pl.ds(r * NU + i * 4 + s, 1), :]
                    t = jnp.tanh(y)
                    h = y + y * t
                    d2 = (1.0 + t) + h * (1.0 - t)
                    pg = hg[:, s * H : (s + 1) * H] * d2
                    sums[s] = sums[s] + jnp.sum(pg.reshape(CH // 8, 8, H), 0)
                    total = pg if total is None else total + pg
                si[at, :] = si[at, :] + total
            for s in range(4):
                up[i * 4 + s] = sums[s]
            return carry

        lax.fori_loop(0, NU // 4, bwd, 0)
        us[pl.ds(r * NU, NU), :] = jnp.sum(up[...], 1)
        s_hi, s_lo = split(si[...])
        ip = mm_nt(s_hi, wi_hi) + mm_nt(s_lo, wi_hi) + mm_nt(s_hi, wi_lo)
        p_hi, p_lo = split(ip)
        gt_total = gt_total + mm(hot, p_hi) + mm(hot, p_lo)

    u_hi, u_lo = split(us[...])
    rows = iota((n * 8, R * NU), 0)
    cols = iota((n * 8, R * NU), 1)
    owner, slot = rows // 8, rows % 8
    perm = (cols == (slot // UL) * NU + owner * UL + slot % UL).astype(F32).astype(BF16)
    o_hi, o_lo = mm(perm, u_hi).astype(BF16), mm(perm, u_lo).astype(BF16)
    w2_hi = jnp.concatenate([wi_hi.astype(F32), jnp.zeros((128 - G, H), F32)], 0).astype(BF16)
    w2_lo = jnp.concatenate([wi_lo.astype(F32), jnp.zeros((128 - G, H), F32)], 0).astype(BF16)
    ugp = mm_nt(o_hi, w2_hi) + mm_nt(o_lo, w2_hi) + mm_nt(o_hi, w2_lo)
    ugs[...] = ugp.reshape(n, 8, 128)
    rug[me] = ugs[me]
    each_peer(gates_copy, start)

    gt_ref[...] = gt_total
    tg = None
    for r in range(R):
        part = mm(cgt[r], ubig[r])
        tg = part if tg is None else tg + part
    tg_ref[...] = tg * scale

    for r in range(R):
        each_peer(grads_copy(r), wait_recv)
        zo_ref[r] = jnp.sum(rz[r].astype(F32), 0)
    each_peer(gates_copy, wait_recv)
    ugo_ref[...] = jnp.sum(rug[...], 0)
    each_peer(users_copy, wait_send)
    for r in range(R):
        each_peer(stats_copy(r), wait_send)
        each_peer(grads_copy(r), wait_send)
    each_peer(gates_copy, wait_send)


def body(
    n,
    user_emb,
    user_gate,
    item_table,
    item_gate,
    cand_ids,
    positives,
    loss_weight,
    w_in,
    b_in,
    w_out,
    b_out,
):
    R, UL, E = user_emb.shape
    G = user_gate.shape[2]
    NU = positives.shape[1]
    C = cand_ids.shape[1]
    T = item_table.shape[0]
    H, K = w_out.shape
    D = E // K
    assert R * UL == 8 and UL * K == 16 and NU == UL * n
    flat = user_emb.reshape(R * UL, E)
    low = jnp.concatenate([flat[:, : E // 2], jnp.pad(user_gate.reshape(R * UL, G), ((0, 0), (0, 128 - G)))], 1)
    high = jnp.pad(flat[:, E // 2 :], ((0, 0), (0, 128)))
    x = jnp.concatenate([low, high], 0)
    dims = (R, NU, UL, C, T, K, E, G, H)
    vm = pl.BlockSpec(memory_space=pltpu.VMEM)
    dma = pltpu.SemaphoreType.DMA
    z, ug, tg, gt = pl.pallas_call(
        functools.partial(kernel, n, dims),
        out_shape=(
            jax.ShapeDtypeStruct((R, UL * K, D), F32),
            jax.ShapeDtypeStruct((R * UL, 128), F32),
            jax.ShapeDtypeStruct((T, E), F32),
            jax.ShapeDtypeStruct((T, G), F32),
        ),
        in_specs=[vm] * 10,
        out_specs=(vm,) * 4,
        scratch_shapes=[
            pltpu.VMEM((n, 16, E // 2 + 128), BF16),
            pltpu.VMEM((R, NU * K, E), BF16),
            pltpu.VMEM((R, C, E), BF16),
            pltpu.VMEM((R, C, H), F32),
            pltpu.VMEM((R * NU, H), F32),
            pltpu.VMEM((R, NU * K, C), F32),
            pltpu.VMEM((R, NU * K, C), F32),
            pltpu.VMEM((R, NU, C), F32),
            pltpu.VMEM((R, 8, 128), F32),
            pltpu.VMEM((R, n, 8, 128), F32),
            pltpu.VMEM((C, NU * 4 * K), BF16),
            pltpu.VMEM((R, T, NU * K), BF16),
            pltpu.VMEM((C, H), F32),
            pltpu.VMEM((NU, 8, H), F32),
            pltpu.VMEM((R * NU, H), F32),
            pltpu.VMEM((R, n, UL * K, D), BF16),
            pltpu.VMEM((R, n, UL * K, D), BF16),
            pltpu.VMEM((n, 8, 128), F32),
            pltpu.VMEM((n, 8, 128), F32),
            dma((n,)),
            dma((n,)),
            dma((R, n)),
            dma((R, n)),
            dma((R, n)),
            dma((R, n)),
            dma((n,)),
            dma((n,)),
        ],
        compiler_params=pltpu.CompilerParams(
            collective_id=0, has_side_effects=True, vmem_limit_bytes=60 * 1024 * 1024
        ),
    )(
        x,
        item_table,
        item_gate,
        cand_ids,
        positives,
        loss_weight,
        w_in,
        b_in.reshape(1, H),
        w_out.T,
        b_out.reshape(1, K),
    )
    return (
        z.reshape(R, UL, E),
        ug[:, :G].reshape(R, UL, G),
        tg,
        gt,
    )


def solution(mesh):
    return jax.shard_map(
        functools.partial(body, mesh.shape["items"]),
        mesh=mesh,
        in_specs=(
            P(None, ("parts", "items"), None),
            P(None, ("parts", "items"), None),
            P(("parts", "items"), None),
            P(("parts", "items"), None),
            P(None, ("parts", "items")),
            P(None, "parts"),
            P(None, "parts"),
            P(),
            P(),
            P(),
            P(),
        ),
        out_specs=(
            P(None, ("parts", "items"), None),
            P(None, ("parts", "items"), None),
            P(("parts", "items"), None),
            P(("parts", "items"), None),
        ),
        check_vma=False,
    )
```

time: 339 us -> 66.9 us (0.20)
  blocking collectives: 161 us -> 0 us
  matrix products: 73.2 us -> 0 us
  Pallas kernels: 0 us -> 54.6 us
  other arithmetic: 53 us -> 1.3 us
  local copies, waits for them, and re-layouts: 32.7 us -> 9.87 us
  between operations: 16.2 us -> 0.65 us
    dot_general x36 -> x0, matrix products: 73.2 us -> none  [the longest x4 35.2 us: one_round(): jnp.einsum('kui,hk->uih', gate_grad, w_out, precision=lax.Precision.HIGHEST)]
    unnamed x1 -> x0, blocking collectives: 58 us -> none
    pallas_call x0 -> x1, Pallas kernels: none -> 54.6 us  [body(): pl.pallas_call(functools.partial(kernel, n, dims), out_shape=(jax.ShapeDt...]
    all_gather x2 -> x0, blocking collectives: 41.3 us -> none  [the longest x1 23.8 us: body(): lax.all_gather(user_emb, 'items', axis=1, tiled=True)]
    pmax x1 -> x0, blocking collectives: 31.1 us -> none  [normaliser(): top = lax.pmax(jnp.max(score, 1), 'items')]
    psum x1 -> x0, blocking collectives: 30.2 us -> none  [normaliser(): total = lax.psum(jnp.sum(jnp.exp(score - top[:, None]), 1), 'items')]
    scatter-add x8 -> x0, other arithmetic: 25.4 us -> none  [the longest x4 16.3 us: body(): table_grad = table_grad.at[local_rows[turn]].add(item_part)]
    sub x5 -> x0, other arithmetic: 18.4 us -> none  [the longest x4 17.9 us: forward(): gates = jax.nn.softmax(gate_logit, axis=0)]
  transfers between devices with their start and end apart: 1 -> 0, of which waited for: 0 -> 0; matrix products, arithmetic and copies ran while one was open for 23% -> 0% of each run, Pallas kernels for 0% -> 0%
where the time goes in v1:
time: 66.9 us; the launch traced here: 66.4 us
  Pallas kernels  54.6 us (82%)
  local copies, waits for them, and re-layouts  9.87 us (15%)
  other arithmetic  1.3 us (2%)
    pallas_call x1, Pallas kernels, body(): pl.pallas_call(functools.partial(kernel, n, dims), out_shape=(jax.ShapeDt...  54.6 us
    unnamed x4, local copies, waits for them, and re-layouts  7.74 us
    reshape x1, local copies, waits for them, and re-layouts, body(): return (z.reshape(R, UL, E), ug[:, :G].reshape(R, UL, G), tg, gt)  1.39 us

profile of v1, /device:TPU:0, one launch (start us, length us, event | category | flops | bytes accessed | tf_op | source)
XLA Modules:
  0.0 66.4 jit_solution(11320795891948044269)
XLA Ops:
  0.6 0.7 %reshape.26 = bf16[8,1024]{1,0:T(8,128)(2,1)S(1)} reshape(bf16[4,2,1024]{2,1,0:T(2,128)(2,1)} %param.11) | data formatting | bytes 32768 | tf_op jit(solution)/shard_map/reshape | solution.py:351
  1.4 1.3 %fusion.4.x_ref = bf16[16,640]{1,0:T(8,128)(2,1)} fusion(bf16[8,512]{1,0:T(8,128)(2,1)S(1)} %get-tuple-element.17, bf16[8,64]{1,0:T(8,128)(2,1)} %bitcast.8, bf16[8,512]{1,0:T(8,128)(2,1)S(1)} %get-tuple-element.16), kind=kLoop, calls=%fused_computation.7 | loop fusion | flops 133120 | bytes 37888 | tf_op jit(solution)/shard_map/concatenate | solution.py:354
  2.7 1.6 %copy.15.ig_ref = bf16[512,64]{1,0:T(8,128)(2,1)} copy(bf16[512,64]{0,1:T(8,128)(2,1)} %param.14) | data formatting | bytes 131072 | tf_op args[3]
  4.3 54.6 %shard_map.138 = (f32[4,16,128]{2,1,0:T(8,128)}, f32[8,128]{1,0:T(8,128)}, f32[512,1024]{1,0:T(8,128)}, f32[512,64]{1,0:T(8,128)}) custom-call(bf16[16,640]{1,0:T(8,128)(2,1)} %fusion.4.x_ref, bf16[512,1024]{1,0:T(8,128)(2,1)} %tab_ref.1, bf16[512,64]{1,0:T(8,128)(2,1)} %copy.15.ig_ref, s32[4,256]{1,0:T(4,128)} %ids_ref.1, s32[4,32]{1,0:T(4,128)} %pos_ref.1, ...), custom_call_target="tpu_custom_call" | custom-call | tf_op jit(solution)/shard_map/pallas_call | solution.py:358
  58.9 1.4 %reshape.30 = f32[4,2,1024]{2,1,0:T(2,128)} reshape(f32[4,16,128]{2,1,0:T(8,128)} %get-tuple-element.8) | data formatting | bytes 65536 | tf_op jit(solution)/shard_map/reshape | solution.py:413
  60.3 1.7 %copy.16 = f32[512,64]{0,1:T(8,128)} copy(f32[512,64]{1,0:T(8,128)} %get-tuple-element.15) | data formatting | bytes 262144
  62.0 1.3 %copy.19 = f32[4,2,64]{2,1,0:T(2,128)} copy(f32[4,2,64]{2,1,0:T(2,128)} %bitcast.7) | data formatting | bytes 4096
  63.3 3.2 %copy.20 = f32[512,1024]{1,0:T(8,128)} copy(f32[512,1024]{1,0:T(8,128)} %get-tuple-element.24) | data formatting | bytes 4194304
  (1 shorter events, 0.0 us)

commit v2 on v1

--- a/solution.py
+++ b/solution.py
@@ -93,61 +93,35 @@
     scale = 1.0 / math.sqrt(D)
     me = lax.axis_index("items")
 
-    def each_peer(make, act):
+    def around(d):
+        peer = me + d
+        return jnp.where(peer >= n, peer - n, peer)
+
+    def send(src, dst, ss, rs):
         def step(d, carry):
-            act(make(d, lax.rem(me + d, n)))
+            peer = around(d)
+            pltpu.make_async_remote_copy(
+                src(peer), dst, ss, rs, device_id={"items": peer}, device_id_type=MESH
+            ).start()
             return carry
 
         lax.fori_loop(1, n, step, 0)
 
-    def users_copy(d, peer):
-        return pltpu.make_async_remote_copy(
-            x_ref, ru.at[me], u_ss.at[d], u_rs.at[d], device_id={"items": peer}, device_id_type=MESH
-        )
-
-    def stats_copy(r):
-        return lambda d, peer: pltpu.make_async_remote_copy(
-            st_out.at[r],
-            st_in.at[r, me],
-            s_ss.at[r, d],
-            s_rs.at[r, d],
-            device_id={"items": peer},
-            device_id_type=MESH,
-        )
-
-    def grads_copy(r):
-        return lambda d, peer: pltpu.make_async_remote_copy(
-            zs.at[r, peer],
-            rz.at[r, me],
-            z_ss.at[r, d],
-            z_rs.at[r, d],
-            device_id={"items": peer},
-            device_id_type=MESH,
-        )
-
-    def gates_copy(d, peer):
-        return pltpu.make_async_remote_copy(
-            ugs.at[peer], rug.at[me], g_ss.at[d], g_rs.at[d], device_id={"items": peer}, device_id_type=MESH
-        )
-
-    def start(c):
-        c.start()
-
-    def wait_recv(c):
-        c.wait_recv()
-
-    def wait_send(c):
-        c.wait_send()
+    def await_all(blocks, sem):
+        pltpu.make_async_copy(blocks, blocks, sem).wait()
+
+    others = pl.ds(0, n - 1)
+    groups = ((0, R - 1), (R - 1, 1)) if R > 1 else ((0, R),)
 
     barrier = pltpu.get_barrier_semaphore()
 
     def greet(d, carry):
-        pl.semaphore_signal(barrier, inc=1, device_id={"items": lax.rem(me + d, n)}, device_id_type=MESH)
+        pl.semaphore_signal(barrier, inc=1, device_id={"items": around(d)}, device_id_type=MESH)
         return carry
 
     lax.fori_loop(1, n, greet, 0)
     pl.semaphore_wait(barrier, n - 1)
-    each_peer(users_copy, start)
+    send(lambda peer: x_ref, ru.at[me], u_ss, u_rs)
     ru[me] = x_ref[...]
 
     w_in = win_ref[...]
@@ -162,10 +136,10 @@
         col = to_col(row, C).astype(jnp.int32)
         pick = (iota((C, T), 1) == jnp.broadcast_to(col, (C, T))).astype(F32).astype(BF16)
         vals[r] = mm(pick, tab_ref[...]).astype(BF16)
-        q = mm(pick, ig_ref[...]).astype(BF16)
+        q = mm_nt(pick, ig_ref[...]).astype(BF16)
         iact[r] = 0.5 * (mm(q, wi_hi) + mm(q, wi_lo))
 
-    each_peer(users_copy, wait_recv)
+    await_all(ru.at[others], u_rs)
 
     packed = ru[...].reshape(n * 16, HALF + 128)
     rows = iota((R * NU, n * 16), 0)
@@ -220,8 +194,11 @@
         ltot = jnp.sum(jnp.exp(score - ltop), 1, keepdims=True)
         st = jnp.where(iota((8, 128), 0) == 0, to_row(ltop, 128), to_row(ltot, 128))
         st_out[r] = st
-        st_in[r, me] = st
-        each_peer(stats_copy(r), start)
+        st_in[me, r] = st
+        for g, (r0, cnt) in enumerate(groups):
+            if r == r0 + cnt - 1:
+                at = pl.ds(r0, cnt)
+                send(lambda peer: st_out.at[at], st_in.at[me, at], s_ss.at[g], s_rs.at[g])
 
     whid = jnp.concatenate([wo_hi, wo_hi, wo_lo, wo_lo], 0) * 0.5
     whid = jnp.concatenate([whid] * 4, 0)
@@ -230,10 +207,12 @@
     whid = jnp.where(keep, whid, 0.0).astype(BF16)
     eye = (iota((C, C), 0) == iota((C, C), 1)).astype(F32).astype(BF16)
     CH = 64
-    gt_total = jnp.zeros((T, G), F32)
+    gt_total = jnp.zeros((G, T), F32)
     for r in range(R):
-        each_peer(stats_copy(r), wait_recv)
-        st = st_in[r]
+        for g, (r0, cnt) in enumerate(groups):
+            if r == r0:
+                await_all(st_in.at[others, pl.ds(r0, cnt)], s_rs.at[g])
+        st = st_in[:, r]
         tops, tots = st[:, 0, :], st[:, 1, :]
         top = jnp.max(tops, 0, keepdims=True)
         tot = jnp.sum(tots * jnp.exp(tops - top), 0, keepdims=True)
@@ -258,9 +237,12 @@
         for k in range(K):
             z = jnp.where(kk == k, wide[:, k * D : (k + 1) * D], z)
         zb = (z * scale).astype(BF16).reshape(n, UL * K, D)
-        zs[r] = zb
-        rz[r, me] = zs[r, me]
-        each_peer(grads_copy(r), start)
+        zs[:, r] = zb
+        rz[me, r] = zs[me, r]
+        for g, (r0, cnt) in enumerate(groups):
+            if r == r0 + cnt - 1:
+                at = pl.ds(r0, cnt)
+                send(lambda peer: zs.at[peer, at], rz.at[me, at], z_ss.at[g], z_rs.at[g])
 
         hot = onehot_cols(r)
         cgt[r] = mm_nt(hot, cgb).astype(BF16)
@@ -290,9 +272,9 @@
         lax.fori_loop(0, NU // 4, bwd, 0)
         us[pl.ds(r * NU, NU), :] = jnp.sum(up[...], 1)
         s_hi, s_lo = split(si[...])
-        ip = mm_nt(s_hi, wi_hi) + mm_nt(s_lo, wi_hi) + mm_nt(s_hi, wi_lo)
+        ip = mm_nt(wi_hi, s_hi) + mm_nt(wi_hi, s_lo) + mm_nt(wi_lo, s_hi)
         p_hi, p_lo = split(ip)
-        gt_total = gt_total + mm(hot, p_hi) + mm(hot, p_lo)
+        gt_total = gt_total + mm_nt(p_hi, hot) + mm_nt(p_lo, hot)
 
     u_hi, u_lo = split(us[...])
     rows = iota((n * 8, R * NU), 0)
@@ -305,7 +287,7 @@
     ugp = mm_nt(o_hi, w2_hi) + mm_nt(o_lo, w2_hi) + mm_nt(o_hi, w2_lo)
     ugs[...] = ugp.reshape(n, 8, 128)
     rug[me] = ugs[me]
-    each_peer(gates_copy, start)
+    send(lambda peer: ugs.at[peer], rug.at[me], g_ss, g_rs)
 
     gt_ref[...] = gt_total
     tg = None
@@ -314,16 +296,17 @@
         tg = part if tg is None else tg + part
     tg_ref[...] = tg * scale
 
-    for r in range(R):
-        each_peer(grads_copy(r), wait_recv)
-        zo_ref[r] = jnp.sum(rz[r].astype(F32), 0)
-    each_peer(gates_copy, wait_recv)
+    for g, (r0, cnt) in enumerate(groups):
+        await_all(rz.at[others, pl.ds(r0, cnt)], z_rs.at[g])
+        for r in range(r0, r0 + cnt):
+            zo_ref[r] = jnp.sum(rz[:, r].astype(F32), 0)
+    await_all(rug.at[others], g_rs)
     ugo_ref[...] = jnp.sum(rug[...], 0)
-    each_peer(users_copy, wait_send)
-    for r in range(R):
-        each_peer(stats_copy(r), wait_send)
-        each_peer(grads_copy(r), wait_send)
-    each_peer(gates_copy, wait_send)
+    await_all(ru.at[others], u_ss)
+    for g, (r0, cnt) in enumerate(groups):
+        await_all(st_in.at[others, pl.ds(r0, cnt)], s_ss.at[g])
+        await_all(zs.at[others, pl.ds(r0, cnt)], z_ss.at[g])
+    await_all(ugs.at[others], g_ss)
 
 
 def body(
@@ -361,7 +344,7 @@
             jax.ShapeDtypeStruct((R, UL * K, D), F32),
             jax.ShapeDtypeStruct((R * UL, 128), F32),
             jax.ShapeDtypeStruct((T, E), F32),
-            jax.ShapeDtypeStruct((T, G), F32),
+            jax.ShapeDtypeStruct((G, T), F32),
         ),
         in_specs=[vm] * 10,
         out_specs=(vm,) * 4,
@@ -375,24 +358,24 @@
             pltpu.VMEM((R, NU * K, C), F32),
             pltpu.VMEM((R, NU, C), F32),
             pltpu.VMEM((R, 8, 128), F32),
-            pltpu.VMEM((R, n, 8, 128), F32),
+            pltpu.VMEM((n, R, 8, 128), F32),
             pltpu.VMEM((C, NU * 4 * K), BF16),
             pltpu.VMEM((R, T, NU * K), BF16),
             pltpu.VMEM((C, H), F32),
             pltpu.VMEM((NU, 8, H), F32),
             pltpu.VMEM((R * NU, H), F32),
-            pltpu.VMEM((R, n, UL * K, D), BF16),
-            pltpu.VMEM((R, n, UL * K, D), BF16),
+            pltpu.VMEM((n, R, UL * K, D), BF16),
+            pltpu.VMEM((n, R, UL * K, D), BF16),
             pltpu.VMEM((n, 8, 128), F32),
             pltpu.VMEM((n, 8, 128), F32),
-            dma((n,)),
-            dma((n,)),
-            dma((R, n)),
-            dma((R, n)),
-            dma((R, n)),
-            dma((R, n)),
-            dma((n,)),
-            dma((n,)),
+            dma,
+            dma,
+            dma((2,)),
+            dma((2,)),
+            dma((2,)),
+            dma((2,)),
+            dma,
+            dma,
         ],
         compiler_params=pltpu.CompilerParams(
             collective_id=0, has_side_effects=True, vmem_limit_bytes=60 * 1024 * 1024
@@ -400,7 +383,7 @@
     )(
         x,
         item_table,
-        item_gate,
+        item_gate.T,
         cand_ids,
         positives,
         loss_weight,
@@ -413,7 +396,7 @@
         z.reshape(R, UL, E),
         ug[:, :G].reshape(R, UL, G),
         tg,
-        gt,
+        gt.T,
     )
 
 

time: 66.9 us -> 61.2 us (0.915)
  Pallas kernels: 54.6 us -> 51.7 us
  local copies, waits for them, and re-layouts: 9.87 us -> 7.25 us
    pallas_call x1, Pallas kernels: 54.6 us -> 51.7 us  [body(): pl.pallas_call(functools.partial(kernel, n, dims), out_shape=(jax.ShapeDt...]
    unnamed x4 -> x5, local copies, waits for them, and re-layouts: 7.74 us -> 5.12 us
where the time goes in v2:
time: 61.2 us; the launch traced here: 60.9 us
  Pallas kernels  51.7 us (84%)
  local copies, waits for them, and re-layouts  7.25 us (12%)
  other arithmetic  1.3 us (2%)
  between operations  0.65 us (1%)
    pallas_call x1, Pallas kernels, body(): pl.pallas_call(functools.partial(kernel, n, dims), out_shape=(jax.ShapeDt...  51.7 us
    unnamed x5, local copies, waits for them, and re-layouts  5.12 us
    reshape x1, local copies, waits for them, and re-layouts, body(): return (z.reshape(R, UL, E), ug[:, :G].reshape(R, UL, G), tg, gt.T)  1.39 us
    concatenate x1, other arithmetic, body(): x = jnp.concatenate([low, high], 0)  1.3 us

profile of v2, /device:TPU:0, one launch (start us, length us, event | category | flops | bytes accessed | tf_op | source)
XLA Modules:
  0.0 60.9 jit_solution(12096962924513341052)
XLA Ops:
  0.6 0.7 %reshape.26 = bf16[8,1024]{1,0:T(8,128)(2,1)S(1)} reshape(bf16[4,2,1024]{2,1,0:T(2,128)(2,1)} %param.11) | data formatting | bytes 32768 | tf_op jit(solution)/shard_map/reshape | solution.py:334
  1.4 1.3 %fusion.4.x_ref = bf16[16,640]{1,0:T(8,128)(2,1)} fusion(bf16[8,512]{1,0:T(8,128)(2,1)S(1)} %get-tuple-element.13, bf16[8,64]{1,0:T(8,128)(2,1)} %bitcast.12, bf16[8,512]{1,0:T(8,128)(2,1)S(1)} %get-tuple-element.12), kind=kLoop, calls=%fused_computation.7 | loop fusion | flops 133120 | bytes 37888 | tf_op jit(solution)/shard_map/concatenate | solution.py:337
  2.7 51.7 %shard_map.138 = (f32[4,16,128]{2,1,0:T(8,128)}, f32[8,128]{1,0:T(8,128)}, f32[512,1024]{1,0:T(8,128)}, f32[64,512]{1,0:T(8,128)}) custom-call(bf16[16,640]{1,0:T(8,128)(2,1)} %fusion.4.x_ref, bf16[512,1024]{1,0:T(8,128)(2,1)} %tab_ref.1, bf16[64,512]{1,0:T(8,128)(2,1)} %bitcast.9, s32[4,256]{1,0:T(4,128)} %ids_ref.1, s32[4,32]{1,0:T(4,128)} %pos_ref.1, ...), custom_call_target="tpu_custom_call" | custom-call | tf_op jit(solution)/shard_map/pallas_call | solution.py:341
  54.4 1.4 %reshape.30 = f32[4,2,1024]{2,1,0:T(2,128)} reshape(f32[4,16,128]{2,1,0:T(8,128)} %get-tuple-element.8) | data formatting | bytes 65536 | tf_op jit(solution)/shard_map/reshape | solution.py:396
  55.7 1.3 %copy.18 = f32[4,2,64]{2,1,0:T(2,128)} copy(f32[4,2,64]{2,1,0:T(2,128)} %bitcast.11) | data formatting | bytes 4096
  57.0 0.0 copy-start
  57.0 3.2 %copy.19 = f32[512,1024]{1,0:T(8,128)} copy(f32[512,1024]{1,0:T(8,128)} %get-tuple-element.20) | data formatting | bytes 4194304
  60.2 0.0 copy-done
  60.2 0.7 %copy.20 = f32[512,64]{0,1:T(8,128)} copy(f32[512,64]{0,1:T(8,128)S(1)} %bitcast.8) | data formatting | bytes 262144
  (1 shorter events, 0.0 us)
Async XLA Ops:
  57.0 3.2 %copy-start = (f32[64,512]{1,0:T(8,128)S(1)}, f32[64,512]{1,0:T(8,128)}, u32[]{:S(2)}) copy-start(f32[64,512]{1,0:T(8,128)} %get-tuple-element.11) | copy-start | bytes 393220

commit v3 on v2

--- a/solution.py
+++ b/solution.py
@@ -120,9 +120,6 @@
         return carry
 
     lax.fori_loop(1, n, greet, 0)
-    pl.semaphore_wait(barrier, n - 1)
-    send(lambda peer: x_ref, ru.at[me], u_ss, u_rs)
-    ru[me] = x_ref[...]
 
     w_in = win_ref[...]
     wi_hi, wi_lo = split(w_in)
@@ -138,6 +135,10 @@
         vals[r] = mm(pick, tab_ref[...]).astype(BF16)
         q = mm_nt(pick, ig_ref[...]).astype(BF16)
         iact[r] = 0.5 * (mm(q, wi_hi) + mm(q, wi_lo))
+        if r == 0:
+            pl.semaphore_wait(barrier, n - 1)
+            send(lambda peer: x_ref, ru.at[me], u_ss, u_rs)
+            ru[me] = x_ref[...]
 
     await_all(ru.at[others], u_rs)
 
@@ -245,7 +246,7 @@
                 send(lambda peer: zs.at[peer, at], rz.at[me, at], z_ss.at[g], z_rs.at[g])
 
         hot = onehot_cols(r)
-        cgt[r] = mm_nt(hot, cgb).astype(BF16)
+        cgt[:, r * NU * K : (r + 1) * NU * K] = mm_nt(hot, cgb).astype(BF16)
 
         si[...] = jnp.zeros_like(si)
 
@@ -290,11 +291,7 @@
     send(lambda peer: ugs.at[peer], rug.at[me], g_ss, g_rs)
 
     gt_ref[...] = gt_total
-    tg = None
-    for r in range(R):
-        part = mm(cgt[r], ubig[r])
-        tg = part if tg is None else tg + part
-    tg_ref[...] = tg * scale
+    tg_ref[...] = mm(cgt[...], ubig[...].reshape(R * NU * K, E)) * scale
 
     for g, (r0, cnt) in enumerate(groups):
         await_all(rz.at[others, pl.ds(r0, cnt)], z_rs.at[g])
@@ -360,7 +357,7 @@
             pltpu.VMEM((R, 8, 128), F32),
             pltpu.VMEM((n, R, 8, 128), F32),
             pltpu.VMEM((C, NU * 4 * K), BF16),
-            pltpu.VMEM((R, T, NU * K), BF16),
+            pltpu.VMEM((T, R * NU * K), BF16),
             pltpu.VMEM((C, H), F32),
             pltpu.VMEM((NU, 8, H), F32),
             pltpu.VMEM((R * NU, H), F32),

time: 61.2 us -> 61.2 us (level)
  no operation moved by 1% of the time
where the time goes in v3:
time: 61.2 us; the launch traced here: 60.9 us
  Pallas kernels  51.7 us (84%)
  local copies, waits for them, and re-layouts  7.25 us (12%)
  other arithmetic  1.3 us (2%)
  between operations  0.65 us (1%)
    pallas_call x1, Pallas kernels, body(): pl.pallas_call(functools.partial(kernel, n, dims), out_shape=(jax.ShapeDt...  51.7 us
    unnamed x5, local copies, waits for them, and re-layouts  5.12 us
    reshape x1, local copies, waits for them, and re-layouts, body(): return (z.reshape(R, UL, E), ug[:, :G].reshape(R, UL, G), tg, gt.T)  1.39 us
    concatenate x1, other arithmetic, body(): x = jnp.concatenate([low, high], 0)  1.3 us

profile of v3, /device:TPU:0, one launch (start us, length us, event | category | flops | bytes accessed | tf_op | source)
XLA Modules:
  0.0 60.9 jit_solution(7545983862119103008)
XLA Ops:
  0.6 0.7 %reshape.26 = bf16[8,1024]{1,0:T(8,128)(2,1)S(1)} reshape(bf16[4,2,1024]{2,1,0:T(2,128)(2,1)} %param.11) | data formatting | bytes 32768 | tf_op jit(solution)/shard_map/reshape | solution.py:331
  1.4 1.3 %fusion.4.x_ref = bf16[16,640]{1,0:T(8,128)(2,1)} fusion(bf16[8,512]{1,0:T(8,128)(2,1)S(1)} %get-tuple-element.13, bf16[8,64]{1,0:T(8,128)(2,1)} %bitcast.12, bf16[8,512]{1,0:T(8,128)(2,1)S(1)} %get-tuple-element.12), kind=kLoop, calls=%fused_computation.7 | loop fusion | flops 133120 | bytes 37888 | tf_op jit(solution)/shard_map/concatenate | solution.py:334
  2.7 51.7 %shard_map.138 = (f32[4,16,128]{2,1,0:T(8,128)}, f32[8,128]{1,0:T(8,128)}, f32[512,1024]{1,0:T(8,128)}, f32[64,512]{1,0:T(8,128)}) custom-call(bf16[16,640]{1,0:T(8,128)(2,1)} %fusion.4.x_ref, bf16[512,1024]{1,0:T(8,128)(2,1)} %tab_ref.1, bf16[64,512]{1,0:T(8,128)(2,1)} %bitcast.9, s32[4,256]{1,0:T(4,128)} %ids_ref.1, s32[4,32]{1,0:T(4,128)} %pos_ref.1, ...), custom_call_target="tpu_custom_call" | custom-call | tf_op jit(solution)/shard_map/pallas_call | solution.py:338
  54.4 1.4 %reshape.30 = f32[4,2,1024]{2,1,0:T(2,128)} reshape(f32[4,16,128]{2,1,0:T(8,128)} %get-tuple-element.8) | data formatting | bytes 65536 | tf_op jit(solution)/shard_map/reshape | solution.py:393
  55.8 1.3 %copy.18 = f32[4,2,64]{2,1,0:T(2,128)} copy(f32[4,2,64]{2,1,0:T(2,128)} %bitcast.11) | data formatting | bytes 4096
  57.0 0.0 copy-start
  57.0 3.2 %copy.19 = f32[512,1024]{1,0:T(8,128)} copy(f32[512,1024]{1,0:T(8,128)} %get-tuple-element.20) | data formatting | bytes 4194304
  60.2 0.0 copy-done
  60.2 0.7 %copy.20 = f32[512,64]{0,1:T(8,128)} copy(f32[512,64]{0,1:T(8,128)S(1)} %bitcast.8) | data formatting | bytes 262144
  (1 shorter events, 0.0 us)
Async XLA Ops:
  57.0 3.2 %copy-start = (f32[64,512]{1,0:T(8,128)S(1)}, f32[64,512]{1,0:T(8,128)}, u32[]{:S(2)}) copy-start(f32[64,512]{1,0:T(8,128)} %get-tuple-element.11) | copy-start | bytes 393220
